TPU v7x, 512 devices: a whole 4x8x8 slice. The times are simulated.
512 devices in a mesh: row: 16 (over y, x_hi), col: 2 (over core), depth: 16 (over z, x_lo).
Axes of the slice: x: 4 (x_hi: 2, x_lo: 2; x = x_hi * 2 + x_lo), y: 8, z: 8, core: 2. Of those that a mesh axis runs over, the one named last changes fastest.
Arguments:
- y_blocks: float32 [4096, 4096], P('row', 'col'), may hold values from -6 to 6
- z_blocks: float32 [4096, 4096], P('row', 'col'), may hold values from -0.125 to 0.125
- h_blocks: float32 [4096, 4096], P('row', 'col'), may hold values from -0.125 to 0.125
- s_pattern: int32 [16, 16], replicated, may hold values 0 or 1
- h_pattern: int32 [16, 16], replicated, may hold values 0 or 1
- keep_mask: int32 [16, 16], replicated, may hold values 0 or 1
Outputs:
- z_next: float32 [4096, 4096], P('row', 'col')
- h_times_z: float32 [4096, 4096], P('row', 'col')
All inputs are finite; a program needn't handle non-finite values.
Results may differ from a plain program's by a relative error of at most 0.00013.
Values sent between devices are 32-bit elements; how exact they have to be, the bound alone decides.
No kernel may reach another device: no remote copies, remote signals or barrier semaphores. Data moves between devices by JAX's collectives and lax.ppermute only.
A program may use at most 128 MiB of HBM per device.

v0:
```python
import jax
import jax.numpy as jnp
from jax import lax
from jax.sharding import PartitionSpec as P

BLK = 256


def from_root(array, axis, root):
    mine = lax.axis_index(axis) == root
    return lax.psum(jnp.where(mine, array, jnp.zeros_like(array)), axis)


def expand(pattern):
    values = pattern.astype(jnp.float32)
    return jnp.repeat(jnp.repeat(values, BLK, axis=0), BLK, axis=1)


def product(left, right):
    return jnp.dot(left, right, preferred_element_type=jnp.float32, precision=lax.Precision.HIGHEST)


def local(y_blocks, z_blocks, h_blocks, s_pattern, h_pattern, keep_mask):
    nblocks = s_pattern.shape[0]
    row_blocks = y_blocks.shape[0] // BLK
    col_blocks = y_blocks.shape[1] // BLK
    row_at = lax.axis_index("row")
    col_at = lax.axis_index("col")
    layer_at = lax.axis_index("depth")

    def local_tile(pattern):
        return expand(
            lax.dynamic_slice(
                pattern, (row_at * row_blocks, col_at * col_blocks), (row_blocks, col_blocks)
            )
        )

    s_local = local_tile(s_pattern)
    keep_local = local_tile(keep_mask)
    masked_y = y_blocks * s_local
    masked_z = z_blocks * s_local
    masked_h = h_blocks * local_tile(h_pattern)

    def multiply(left, right):
        layers = lax.axis_size("depth")
        inner = nblocks // layers
        lowest = layer_at * inner
        step_width = min(inner, col_blocks, row_blocks)
        inner_at = lowest + 0
        piece_a = lax.dynamic_slice_in_dim(left, inner_at % col_blocks * BLK, step_width * BLK, 1)
        part_a = from_root(piece_a, "col", inner_at // col_blocks)
        part_b = from_root(right, "row", inner_at // row_blocks)
        summed = product(part_a, part_b)
        return summed

    def filter_part(values, row_offset, col_offset):
        keep_part = lax.dynamic_slice(keep_local, (row_offset, col_offset), values.shape)
        return keep_part * values

    def shift_part(values, row_offset, col_offset):
        filtered = filter_part(values, row_offset, col_offset)
        global_rows = (
            row_at * (row_blocks * BLK) + row_offset + jnp.arange(values.shape[0], dtype=jnp.int32)
        )
        global_cols = (
            col_at * (col_blocks * BLK) + col_offset + jnp.arange(values.shape[1], dtype=jnp.int32)
        )
        diagonal_ones = global_rows[:, None] == global_cols[None, :]
        return jnp.where(diagonal_ones, 1.5, 0.0).astype(jnp.float32) - 0.5 * filtered

    def combine_depth(partial_sum, finish):
        share = lax.psum_scatter(partial_sum, "depth", scatter_dimension=0, tiled=True)
        finished = finish(share, layer_at * share.shape[0], 0)
        return lax.all_gather(finished, "depth", axis=0, tiled=True)

    q_matrix = combine_depth(multiply(masked_z, masked_y), shift_part)
    z_next = combine_depth(multiply(q_matrix, masked_z), filter_part)
    h_times_z = combine_depth(multiply(masked_h, z_next), filter_part)
    return (z_next, h_times_z)


def solution(mesh):
    in_specs = (P("row", "col"), P("row", "col"), P("row", "col"), P(), P(), P())
    out_specs = (P("row", "col"), P("row", "col"))
    return jax.shard_map(local, mesh=mesh, in_specs=in_specs, out_specs=out_specs, check_vma=False)
```

profile of v0, /device:TPU:24, one launch (start us, length us, event | category | flops | bytes accessed | tf_op | source)
XLA Modules:
  0.0 970.4 jit_solution(15851494755314473935)
XLA Ops:
  8.1 5.1 broadcast_select_fusion.1
  14.7 38.4 %all-reduce.7.cloned.1.call-done = f32[256,256]{1,0:T(8,128)} async-done(((f32[256,256]{1,0:T(8,128)}), f32[256,256]{1,0:T(8,128)}) %all-reduce.7.cloned.1.call-update) | async-done | bytes 262160 | tf_op jit(solution)/shard_map/psum | solution.py:11
  53.1 217.4 %all-reduce.11.cloned.1.call-done = (f32[256,2048]{1,0:T(8,128)}, f32[256,2048]{1,0:T(8,128)}) async-done(((f32[256,2048]{1,0:T(8,128)}, f32[256,2048]{1,0:T(8,128)}), (f32[256,2048]{1,0:T(8,128)}, f32[256,2048]{1,0:T(8,128)})) %all-reduce.11.cloned.1.call-update) | async-done | bytes 4194320 | tf_op jit(solution)/shard_map/psum | solution.py:11
  270.5 4.9 fusion.1
  275.5 0.9 convert_bitcast_fusion
  276.5 77.8 %reduce-scatter.4.cloned.1.call-done = f32[16,2048]{1,0:T(8,128)} async-done(((f32[256,2048]{1,0:T(8,128)}), f32[16,2048]{1,0:T(8,128)}) %reduce-scatter.4.cloned.1.call-update) | async-done | bytes 131088 | tf_op jit(solution)/shard_map/reduce_scatter | solution.py:72
  354.3 1.6 multiply_subtract_fusion
  356.2 1.7 fusion
  357.8 73.7 %all-gather.4.cloned.1.call-done = f32[256,2048]{1,0:T(8,128)} async-done(((f32[16,2048]{1,0:T(8,128)}), f32[256,2048]{1,0:T(8,128)}) %all-gather.4.cloned.1.call-update) | async-done | bytes 2097168 | tf_op jit(solution)/shard_map/all_gather | solution.py:74
  431.5 1.7 dynamic-slice_select_fusion
  433.3 34.2 %all-reduce.13.cloned.1.call-done = (f32[256,256]{1,0:T(8,128)}, f32[256,256]{1,0:T(8,128)}) async-done(((f32[256,256]{1,0:T(8,128)}, f32[256,256]{1,0:T(8,128)}), (f32[256,256]{1,0:T(8,128)}, f32[256,256]{1,0:T(8,128)})) %all-reduce.13.cloned.1.call-update) | async-done | bytes 524304 | tf_op jit(solution)/shard_map/psum | solution.py:11
  467.5 4.2 fusion.2
  471.8 80.1 %reduce-scatter.6.cloned.1.call-done = f32[16,2048]{1,0:T(8,128)} async-done(((f32[256,2048]{1,0:T(8,128)}), f32[16,2048]{1,0:T(8,128)}) %reduce-scatter.6.cloned.1.call-update) | async-done | bytes 131088 | tf_op jit(solution)/shard_map/reduce_scatter | solution.py:72
  551.9 1.6 broadcast_multiply_fusion.2
  553.5 75.4 %all-gather.6.cloned.1.call-done = f32[256,2048]{1,0:T(8,128)} async-done(((f32[16,2048]{1,0:T(8,128)}), f32[256,2048]{1,0:T(8,128)}) %all-gather.6.cloned.1.call-update) | async-done | bytes 2097168 | tf_op jit(solution)/shard_map/all_gather | solution.py:74
  628.9 1.5 broadcast_select_fusion
  630.5 170.2 %all-reduce.9.cloned.1.call-done = f32[256,2048]{1,0:T(8,128)} async-done(((f32[256,2048]{1,0:T(8,128)}), f32[256,2048]{1,0:T(8,128)}) %all-reduce.9.cloned.1.call-update) | async-done | bytes 2097168 | tf_op jit(solution)/shard_map/psum | solution.py:11
  800.7 4.8 fusion.3
  805.5 77.8 %reduce-scatter.8.cloned.1.call-done = f32[16,2048]{1,0:T(8,128)} async-done(((f32[256,2048]{1,0:T(8,128)}), f32[16,2048]{1,0:T(8,128)}) %reduce-scatter.8.cloned.1.call-update) | async-done | bytes 131088 | tf_op jit(solution)/shard_map/reduce_scatter | solution.py:72
  883.3 1.6 broadcast_multiply_fusion.1
  884.9 75.0 %all-gather.8.cloned.1.call-done = f32[256,2048]{1,0:T(8,128)} async-done(((f32[16,2048]{1,0:T(8,128)}), f32[256,2048]{1,0:T(8,128)}) %all-gather.8.cloned.1.call-update) | async-done | bytes 2097168 | tf_op jit(solution)/shard_map/all_gather | solution.py:74
  959.9 1.3 copy.19
  961.2 1.0 copy-done.2
  962.3 1.3 copy.20
  (38 shorter events, 3.1 us)
Async XLA Ops:
  7.2 45.9 %all-reduce.7.cloned.1.call-start = ((), (), s32[]{:S(2)}) async-start(), calls=%async_computation.3 | async-start | bytes 524288 | tf_op jit(solution)/shard_map/psum | solution.py:11
  13.9 256.6 %all-reduce.11.cloned.1.call-start = ((), (), s32[]{:S(2)}) async-start(), calls=%async_computation.11 | async-start | bytes 8388608 | tf_op jit(solution)/shard_map/psum | solution.py:11
  14.7 339.6 %reduce-scatter.4.cloned.1.call-start = ((), (), s32[]{:S(2)}) async-start(), calls=%async_computation.4 | async-start | bytes 2228224 | tf_op jit(solution)/shard_map/reduce_scatter | solution.py:72
  275.4 192.1 %copy-start.1 = (f32[256,2048]{1,0:T(8,128)S(1)}, f32[256,2048]{1,0:T(8,128)}, u32[]{:S(2)}) copy-start(f32[256,2048]{1,0:T(8,128)} %get-tuple-element.3) | copy-start | bytes 6291460
  275.4 156.1 %all-gather.4.cloned.1.call-start = ((), (), s32[]{:S(2)}) async-start(), calls=%async_computation.5 | async-start | bytes 2228224 | tf_op jit(solution)/shard_map/all_gather | solution.py:74
  356.0 111.5 %all-reduce.13.cloned.1.call-start = ((), (), s32[]{:S(2)}) async-start(), calls=%async_computation.12 | async-start | bytes 1048576 | tf_op jit(solution)/shard_map/psum | solution.py:11
  433.2 118.6 %reduce-scatter.6.cloned.1.call-start = ((), (), s32[]{:S(2)}) async-start(), calls=%async_computation.6 | async-start | bytes 2228224 | tf_op jit(solution)/shard_map/reduce_scatter | solution.py:72
  471.7 157.2 %all-gather.6.cloned.1.call-start = ((), (), s32[]{:S(2)}) async-start(), calls=%async_computation.7 | async-start | bytes 2228224 | tf_op jit(solution)/shard_map/all_gather | solution.py:74
  553.5 247.2 %all-reduce.9.cloned.1.call-start = ((), (), s32[]{:S(2)}) async-start(), calls=%async_computation.8 | async-start | bytes 4194304 | tf_op jit(solution)/shard_map/psum | solution.py:11
  630.5 170.2 %copy-start.3 = (f32[256,256]{1,0:T(8,128)S(1)}, f32[256,256]{1,0:T(8,128)}, u32[]{:S(2)}) copy-start(f32[256,256]{1,0:T(8,128)} %get-tuple-element.5) | copy-start | bytes 786436
  630.5 252.9 %reduce-scatter.8.cloned.1.call-start = ((), (), s32[]{:S(2)}) async-start(), calls=%async_computation.9 | async-start | bytes 2228224 | tf_op jit(solution)/shard_map/reduce_scatter | solution.py:72
  805.5 154.4 %copy-start = (f32[256,2048]{1,0:T(8,128)S(1)}, f32[256,2048]{1,0:T(8,128)}, u32[]{:S(2)}) copy-start(f32[256,2048]{1,0:T(8,128)} %all-gather.6.cloned.1.call-done) | copy-start | bytes 6291460
  805.5 154.4 %all-gather.8.cloned.1.call-start = ((), (), s32[]{:S(2)}) async-start(), calls=%async_computation.10 | async-start | bytes 2228224 | tf_op jit(solution)/shard_map/all_gather | solution.py:74
  959.9 2.3 copy-start.2
Sparse Core Ops, SparseCore 0:
  14.0 39.0 all-reduce.6
  57.0 213.5 all-reduce.10
  275.6 78.6 reduce-scatter.3
  357.0 74.4 all-gather.3
  435.1 32.3 all-reduce.12
  471.8 79.9 reduce-scatter.5
  554.5 74.3 all-gather.5
  632.4 168.2 all-reduce.8
  805.6 77.6 reduce-scatter.7
  885.8 74.0 all-gather.7
where the time goes:
time: 971 us; the launch traced here: 970 us
  waiting for transfers between devices  921 us (95%)
  other arithmetic  17.1 us (2%)
  between operations  14.2 us (1%)
  matrix products  13.9 us (1%)
    psum x4, waiting for transfers between devices, from_root(): return lax.psum(jnp.where(mine, array, jnp.zeros_like(array)), axis)  460 us
    reduce_scatter x3, waiting for transfers between devices, combine_depth(): lax.psum_scatter(partial_sum, 'depth', scatter_dimension=0, tiled=True)  236 us
    all_gather x3, waiting for transfers between devices, combine_depth(): return lax.all_gather(finished, 'depth', axis=0, tiled=True)  224 us
  transfers between devices with their start and end apart: 10, of which 10 were waited for; matrix products, arithmetic and copies ran while one was open for 0% of the time, Pallas kernels for 0%

commit v1 on v0

--- a/solution.py
+++ b/solution.py
@@ -71,7 +71,9 @@
     def combine_depth(partial_sum, finish):
         share = lax.psum_scatter(partial_sum, "depth", scatter_dimension=0, tiled=True)
         finished = finish(share, layer_at * share.shape[0], 0)
-        return lax.all_gather(finished, "depth", axis=0, tiled=True)
+        return jnp.concatenate(
+            lax.all_to_all(jnp.stack([finished] * lax.axis_size("depth")), "depth", 0, 0), axis=0
+        )
 
     q_matrix = combine_depth(multiply(masked_z, masked_y), shift_part)
     z_next = combine_depth(multiply(q_matrix, masked_z), filter_part)

time: 971 us -> 877 us (0.903)
  the two profiles are of different devices: /device:TPU:24 before, /device:TPU:16 now
where the time goes in v1:
time: 877 us
  waiting for transfers between devices  771 us (88%)
  blocking collectives  45.6 us (5%)
  matrix products  14.6 us (2%)
  between operations  14.2 us (2%)
  other arithmetic  14.1 us (2%)
  starting transfers between devices  9.06 us (1%)
    psum x4, waiting for transfers between devices, from_root(): return lax.psum(jnp.where(mine, array, jnp.zeros_like(array)), axis)  457 us
    reduce_scatter x3, waiting for transfers between devices, combine_depth(): lax.psum_scatter(partial_sum, 'depth', scatter_dimension=0, tiled=True)  236 us
    all_to_all x2, waiting for transfers between devices, combine_depth(): lax.all_to_all(jnp.stack([finished] * lax.axis_size('depth')), 'depth', 0...  77.9 us
    all_to_all x1, blocking collectives, combine_depth(): lax.all_to_all(jnp.stack([finished] * lax.axis_size('depth')), 'depth', 0...  45.6 us
  transfers between devices with their start and end apart: 9, of which 9 were waited for; matrix products, arithmetic and copies ran while one was open for 0% of the time, Pallas kernels for 0%

profile of v1, /device:TPU:16, one launch (start us, length us, event | category | flops | bytes accessed | tf_op | source)
XLA Modules:
  0.0 876.8 jit_solution(2311167227745724289)
XLA Ops:
  8.1 5.1 broadcast_select_fusion.1
  14.7 38.5 %all-reduce.7.cloned.1.call-done = f32[256,256]{1,0:T(8,128)} async-done(((f32[256,256]{1,0:T(8,128)}), f32[256,256]{1,0:T(8,128)}) %all-reduce.7.cloned.1.call-update) | async-done | bytes 262160 | tf_op jit(solution)/shard_map/psum | solution.py:11
  53.2 217.3 %all-reduce.11.cloned.1.call-done = (f32[256,2048]{1,0:T(8,128)}, f32[256,2048]{1,0:T(8,128)}) async-done(((f32[256,2048]{1,0:T(8,128)}, f32[256,2048]{1,0:T(8,128)}), (f32[256,2048]{1,0:T(8,128)}, f32[256,2048]{1,0:T(8,128)})) %all-reduce.11.cloned.1.call-update) | async-done | bytes 4194320 | tf_op jit(solution)/shard_map/psum | solution.py:11
  270.5 4.9 fusion.1
  276.3 78.0 %reduce-scatter.4.cloned.1.call-done = f32[16,2048]{1,0:T(8,128)} async-done(((f32[256,2048]{1,0:T(8,128)}), f32[16,2048]{1,0:T(8,128)}) %reduce-scatter.4.cloned.1.call-update) | async-done | bytes 131088 | tf_op jit(solution)/shard_map/reduce_scatter | solution.py:72
  354.3 1.0 multiply_subtract_fusion
  355.3 1.6 stack.6
  356.9 4.2 all-to-all-start
  361.3 1.7 fusion
  363.0 37.8 %all-to-all-done = f32[16,16,2048]{2,1,0:T(8,128)S(1)} async-done(((f32[16,16,2048]{2,1,0:T(8,128)}), f32[16,16,2048]{2,1,0:T(8,128)S(1)}, u32[]{:S(2)}, u32[]{:S(2)}) %all-to-all-start) | async-done | bytes 2097184 | tf_op jit(solution)/shard_map/all_to_all | solution.py:75
  401.6 33.9 %all-reduce.13.cloned.1.call-done = (f32[256,256]{1,0:T(8,128)}, f32[256,256]{1,0:T(8,128)}) async-done(((f32[256,256]{1,0:T(8,128)}, f32[256,256]{1,0:T(8,128)}), (f32[256,256]{1,0:T(8,128)}, f32[256,256]{1,0:T(8,128)})) %all-reduce.13.cloned.1.call-update) | async-done | bytes 524304 | tf_op jit(solution)/shard_map/psum | solution.py:11
  435.5 4.9 fusion.2
  440.4 80.2 %reduce-scatter.6.cloned.1.call-done = f32[16,2048]{1,0:T(8,128)} async-done(((f32[256,2048]{1,0:T(8,128)}), f32[16,2048]{1,0:T(8,128)}) %reduce-scatter.6.cloned.1.call-update) | async-done | bytes 131088 | tf_op jit(solution)/shard_map/reduce_scatter | solution.py:72
  520.7 0.9 broadcast_multiply_fusion.2
  521.8 45.6 %all_to_all.15 = f32[16,16,2048]{2,1,0:T(8,128)S(1)} all-to-all(f32[16,16,2048]{2,1,0:T(8,128)S(1)} %stack.7), channel_id=1, replica_groups=mesh['row'=16,'col'=2,'depth'=16] {'depth'}, dimensions={0} | all-to-all | bytes 4194304 | tf_op jit(solution)/shard_map/all_to_all | solution.py:75
  567.5 1.5 broadcast_select_fusion
  569.1 166.9 %all-reduce.9.cloned.1.call-done = f32[256,2048]{1,0:T(8,128)} async-done(((f32[256,2048]{1,0:T(8,128)}), f32[256,2048]{1,0:T(8,128)}) %all-reduce.9.cloned.1.call-update) | async-done | bytes 2097168 | tf_op jit(solution)/shard_map/psum | solution.py:11
  736.0 4.8 fusion.3
  740.8 77.5 %reduce-scatter.8.cloned.1.call-done = f32[16,2048]{1,0:T(8,128)} async-done(((f32[256,2048]{1,0:T(8,128)}), f32[16,2048]{1,0:T(8,128)}) %reduce-scatter.8.cloned.1.call-update) | async-done | bytes 131088 | tf_op jit(solution)/shard_map/reduce_scatter | solution.py:72
  819.2 1.6 stack.8
  820.8 4.6 all-to-all-start.2
  825.4 40.1 %all-to-all-done.2 = f32[16,16,2048]{2,1,0:T(8,128)} async-done(((f32[16,16,2048]{2,1,0:T(8,128)}), f32[16,16,2048]{2,1,0:T(8,128)}, u32[]{:S(2)}, u32[]{:S(2)}) %all-to-all-start.2) | async-done | bytes 2097184 | tf_op jit(solution)/shard_map/all_to_all | solution.py:75
  865.5 1.3 copy.19
  866.8 3.1 copy.20
  (31 shorter events, 5.6 us)
Async XLA Ops:
  7.2 46.0 %all-reduce.7.cloned.1.call-start = ((), (), s32[]{:S(2)}) async-start(), calls=%async_computation.6 | async-start | bytes 524288 | tf_op jit(solution)/shard_map/psum | solution.py:11
  13.9 256.6 %all-reduce.11.cloned.1.call-start = ((), (), s32[]{:S(2)}) async-start(), calls=%async_computation.11 | async-start | bytes 8388608 | tf_op jit(solution)/shard_map/psum | solution.py:11
  14.7 339.7 %reduce-scatter.4.cloned.1.call-start = ((), (), s32[]{:S(2)}) async-start(), calls=%async_computation.7 | async-start | bytes 2228224 | tf_op jit(solution)/shard_map/reduce_scatter | solution.py:72
  356.9 43.9 %all-to-all-start = ((f32[16,16,2048]{2,1,0:T(8,128)}), f32[16,16,2048]{2,1,0:T(8,128)S(1)}, u32[]{:S(2)}, u32[]{:S(2)}) async-start(f32[16,16,2048]{2,1,0:T(8,128)} %stack.6), calls=%async_computation.1 | async-start | bytes 4194304 | tf_op jit(solution)/shard_map/all_to_all | solution.py:75
  361.1 74.4 %all-reduce.13.cloned.1.call-start = ((), (), s32[]{:S(2)}) async-start(), calls=%async_computation.12 | async-start | bytes 1048576 | tf_op jit(solution)/shard_map/psum | solution.py:11
  401.5 119.1 %reduce-scatter.6.cloned.1.call-start = ((), (), s32[]{:S(2)}) async-start(), calls=%async_computation.8 | async-start | bytes 2228224 | tf_op jit(solution)/shard_map/reduce_scatter | solution.py:72
  440.4 295.6 %all-reduce.9.cloned.1.call-start = ((), (), s32[]{:S(2)}) async-start(), calls=%async_computation.9 | async-start | bytes 4194304 | tf_op jit(solution)/shard_map/psum | solution.py:11
  569.0 167.0 %copy-start = (f32[256,256]{1,0:T(8,128)S(1)}, f32[256,256]{1,0:T(8,128)}, u32[]{:S(2)}) copy-start(f32[256,256]{1,0:T(8,128)} %get-tuple-element.5) | copy-start | bytes 786436
  569.0 249.3 %reduce-scatter.8.cloned.1.call-start = ((), (), s32[]{:S(2)}) async-start(), calls=%async_computation.10 | async-start | bytes 2228224 | tf_op jit(solution)/shard_map/reduce_scatter | solution.py:72
  820.8 44.7 %all-to-all-start.2 = ((f32[16,16,2048]{2,1,0:T(8,128)}), f32[16,16,2048]{2,1,0:T(8,128)}, u32[]{:S(2)}, u32[]{:S(2)}) async-start(f32[16,16,2048]{2,1,0:T(8,128)} %stack.8), calls=%async_computation.5 | async-start | bytes 4194304 | tf_op jit(solution)/shard_map/all_to_all | solution.py:75
Sparse Core Ops, SparseCore 0:
  14.0 39.1 all-reduce.6
  57.0 213.4 all-reduce.10
  275.6 78.7 reduce-scatter.3
  401.7 33.7 all-reduce.12
  440.5 80.1 reduce-scatter.5
  569.1 166.8 all-reduce.8
  740.9 77.3 reduce-scatter.7

commit v2 on v0

--- a/solution.py
+++ b/solution.py
@@ -8,7 +8,7 @@
 
 def from_root(array, axis, root):
     mine = lax.axis_index(axis) == root
-    return lax.psum(jnp.where(mine, array, jnp.zeros_like(array)), axis)
+    return jnp.sum(lax.all_gather(jnp.where(mine, array, jnp.zeros_like(array)), axis), axis=0)
 
 
 def expand(pattern):

time: 971 us -> 1780 us (1.83)
  waiting for transfers between devices: 921 us -> 1690 us
  other arithmetic: 17.1 us -> 51.4 us
    all_gather x0 -> x3, waiting for transfers between devices: none -> 1250 us  [from_root(): lax.all_gather(jnp.where(mine, array, jnp.zeros_like(array)), axis)]
    psum x4 -> x0, waiting for transfers between devices: 460 us -> none  [from_root(): return lax.psum(jnp.where(mine, array, jnp.zeros_like(array)), axis)]
    reduce_sum x0 -> x6, other arithmetic: none -> 35.5 us  [from_root(): jnp.sum(lax.all_gather(jnp.where(mine, array, jnp.zeros_like(array)), axi...]
  transfers between devices with their start and end apart: 10 -> 9, of which waited for: 10 -> 9; matrix products, arithmetic and copies ran while one was open for 0% -> 1% of each run, Pallas kernels for 0% -> 0%
where the time goes in v2:
time: 1780 us
  waiting for transfers between devices  1690 us (95%)
  other arithmetic  51.4 us (3%)
    all_gather x3, waiting for transfers between devices, from_root(): lax.all_gather(jnp.where(mine, array, jnp.zeros_like(array)), axis)  1250 us
    reduce_scatter x3, waiting for transfers between devices, combine_depth(): lax.psum_scatter(partial_sum, 'depth', scatter_dimension=0, tiled=True)  227 us
    all_gather x3, waiting for transfers between devices, combine_depth(): return lax.all_gather(finished, 'depth', axis=0, tiled=True)  215 us
  transfers between devices with their start and end apart: 9, of which 9 were waited for; matrix products, arithmetic and copies ran while one was open for 1% of the time, Pallas kernels for 0%

profile of v2, /device:TPU:24, one launch (start us, length us, event | category | flops | bytes accessed | tf_op | source)
XLA Modules:
  0.0 1779.9 jit_solution(9365834841171555758)
XLA Ops:
  8.1 5.2 broadcast_select_fusion.1
  13.4 2.2 all-gather
  15.6 420.2 %all-gather.19.cloned.1.call-done = f32[4096,2048]{1,0:T(8,128)} async-done(((f32[256,2048]{1,0:T(8,128)}), f32[4096,2048]{1,0:T(8,128)}) %all-gather.19.cloned.1.call-update) | async-done | bytes 33554448 | tf_op jit(solution)/shard_map/all_gather | solution.py:11
  435.9 11.8 reduce_sum.55
  447.7 3.2 fusion.1
  452.6 74.5 %reduce-scatter.4.cloned.1.call-done = f32[16,2048]{1,0:T(8,128)} async-done(((f32[256,2048]{1,0:T(8,128)}), f32[16,2048]{1,0:T(8,128)}) %reduce-scatter.4.cloned.1.call-update) | async-done | bytes 131088 | tf_op jit(solution)/shard_map/reduce_scatter | solution.py:72
  527.1 1.6 multiply_subtract_fusion
  528.8 418.0 %all-gather.21.cloned.1.call-done = f32[4096,2048]{1,0:T(8,128)} async-done(((f32[256,2048]{1,0:T(8,128)}), f32[4096,2048]{1,0:T(8,128)}) %all-gather.21.cloned.1.call-update) | async-done | bytes 33554448 | tf_op jit(solution)/shard_map/all_gather | solution.py:11
  946.8 11.8 reduce_sum.57
  958.6 64.3 %all-gather.13.cloned.1.call-done = f32[256,2048]{1,0:T(8,128)} async-done(((f32[16,2048]{1,0:T(8,128)}), f32[256,2048]{1,0:T(8,128)}) %all-gather.13.cloned.1.call-update) | async-done | bytes 2097168 | tf_op jit(solution)/shard_map/all_gather | solution.py:74
  1023.9 2.2 all-gather.2
  1026.1 3.2 fusion.2
  1029.4 76.1 %reduce-scatter.6.cloned.1.call-done = f32[16,2048]{1,0:T(8,128)} async-done(((f32[256,2048]{1,0:T(8,128)}), f32[16,2048]{1,0:T(8,128)}) %reduce-scatter.6.cloned.1.call-update) | async-done | bytes 131088 | tf_op jit(solution)/shard_map/reduce_scatter | solution.py:72
  1105.4 1.6 broadcast_multiply_fusion.2
  1107.1 75.4 %all-gather.15.cloned.1.call-done = f32[256,2048]{1,0:T(8,128)} async-done(((f32[16,2048]{1,0:T(8,128)}), f32[256,2048]{1,0:T(8,128)}) %all-gather.15.cloned.1.call-update) | async-done | bytes 2097168 | tf_op jit(solution)/shard_map/all_gather | solution.py:74
  1182.5 1.5 broadcast_select_fusion
  1186.0 2.2 all-gather.4
  1188.3 413.2 %all-gather.23.cloned.1.call-done = f32[4096,2048]{1,0:T(8,128)} async-done(((f32[256,2048]{1,0:T(8,128)}), f32[4096,2048]{1,0:T(8,128)}) %all-gather.23.cloned.1.call-update) | async-done | bytes 33554448 | tf_op jit(solution)/shard_map/all_gather | solution.py:11
  1601.4 11.8 reduce_sum.59
  1613.3 3.2 fusion.3
  1616.6 76.3 %reduce-scatter.8.cloned.1.call-done = f32[16,2048]{1,0:T(8,128)} async-done(((f32[256,2048]{1,0:T(8,128)}), f32[16,2048]{1,0:T(8,128)}) %reduce-scatter.8.cloned.1.call-update) | async-done | bytes 131088 | tf_op jit(solution)/shard_map/reduce_scatter | solution.py:72
  1692.8 1.6 broadcast_multiply_fusion.1
  1694.4 75.3 %all-gather.17.cloned.1.call-done = f32[256,2048]{1,0:T(8,128)} async-done(((f32[16,2048]{1,0:T(8,128)}), f32[256,2048]{1,0:T(8,128)}) %all-gather.17.cloned.1.call-update) | async-done | bytes 2097168 | tf_op jit(solution)/shard_map/all_gather | solution.py:74
  1769.7 1.3 copy.13
  (41 shorter events, 8.2 us)
Async XLA Ops:
  7.2 428.7 %all-gather.19.cloned.1.call-start = ((), (), s32[]{:S(2)}) async-start(), calls=%async_computation.9 | async-start | bytes 35651584 | tf_op jit(solution)/shard_map/all_gather | solution.py:11
  13.3 513.8 %reduce-scatter.4.cloned.1.call-start = ((), (), s32[]{:S(2)}) async-start(), calls=%async_computation.3 | async-start | bytes 2228224 | tf_op jit(solution)/shard_map/reduce_scatter | solution.py:72
  450.9 495.8 %all-gather.21.cloned.1.call-start = ((), (), s32[]{:S(2)}) async-start(), calls=%async_computation.10 | async-start | bytes 35651584 | tf_op jit(solution)/shard_map/all_gather | solution.py:11
  451.7 571.2 %all-gather.13.cloned.1.call-start = ((), (), s32[]{:S(2)}) async-start(), calls=%async_computation.4 | async-start | bytes 2228224 | tf_op jit(solution)/shard_map/all_gather | solution.py:74
  528.8 576.7 %reduce-scatter.6.cloned.1.call-start = ((), (), s32[]{:S(2)}) async-start(), calls=%async_computation.5 | async-start | bytes 2228224 | tf_op jit(solution)/shard_map/reduce_scatter | solution.py:72
  1029.3 153.2 %all-gather.15.cloned.1.call-start = ((), (), s32[]{:S(2)}) async-start(), calls=%async_computation.6 | async-start | bytes 2228224 | tf_op jit(solution)/shard_map/all_gather | solution.py:74
  1107.0 494.4 %all-gather.23.cloned.1.call-start = ((), (), s32[]{:S(2)}) async-start(), calls=%async_computation.11 | async-start | bytes 35651584 | tf_op jit(solution)/shard_map/all_gather | solution.py:11
  1184.1 508.7 %reduce-scatter.8.cloned.1.call-start = ((), (), s32[]{:S(2)}) async-start(), calls=%async_computation.7 | async-start | bytes 2228224 | tf_op jit(solution)/shard_map/reduce_scatter | solution.py:72
  1616.5 153.2 %copy-start = (f32[256,2048]{1,0:T(8,128)S(1)}, f32[256,2048]{1,0:T(8,128)}, u32[]{:S(2)}) copy-start(f32[256,2048]{1,0:T(8,128)} %all-gather.15.cloned.1.call-done) | copy-start | bytes 6291460
  1616.5 153.2 %all-gather.17.cloned.1.call-start = ((), (), s32[]{:S(2)}) async-start(), calls=%async_computation.8 | async-start | bytes 2228224 | tf_op jit(solution)/shard_map/all_gather | solution.py:74
  1769.7 2.3 copy-start.1
Sparse Core Ops, SparseCore 0:
  13.4 422.3 all-gather.18
  451.1 75.9 reduce-scatter.3
  530.9 415.8 all-gather.20
  949.3 73.5 all-gather.12
  1029.4 75.9 reduce-scatter.5
  1107.9 74.5 all-gather.14
  1186.3 415.1 all-gather.22
  1616.6 76.1 reduce-scatter.7
  1695.5 74.1 all-gather.16
